TPU v7x, 128 devices: a whole 4x4x4 slice. The times are simulated.
128 devices in a mesh: lat: 4 (over y_hi, core), lon: 32 (over y_lo, z, x).
Axes of the slice: x: 4, y: 4 (y_hi: 2, y_lo: 2; y = y_hi * 2 + y_lo), z: 4, core: 2. Of those that a mesh axis runs over, the one named last changes fastest.
Arguments:
- fields: bfloat16 [12, 96, 30720], P('lat', None, 'lon'), may hold values from -6 to 6
- surface_kind: int32 [96, 384], P('lat', 'lon'), may hold values from 0 to 2
- patch_weight: bfloat16 [80, 512], replicated, may hold values from -0.625 to 0.625
- level_embed: float32 [12, 512], replicated, may hold values from -6 to 6
- enc_gain: float32 [512], replicated, may hold values from 0.1 to 1.9
- latent_query: bfloat16 [3, 512], replicated, may hold values from -6 to 6
- kv_weight: bfloat16 [512, 1024], replicated, may hold values from -0.25 to 0.25
- enc_scale: float32 [8], replicated, may hold values from 0.5 to 100, as said below
- enc_out_weight: bfloat16 [512, 512], replicated, may hold values from -0.25 to 0.25
- kind_embed: float32 [3, 512], replicated, may hold values from -6 to 6
- attn_gain: float32 [512], replicated, may hold values from 0.1 to 1.9
- qkv_weight: bfloat16 [512, 1536], replicated, may hold values from -0.25 to 0.25
- swin_scale: float32 [8], replicated, may hold values from 0.5 to 100, as said below
- proj_weight: bfloat16 [512, 512], replicated, may hold values from -0.25 to 0.25
- mlp_gain: float32 [512], replicated, may hold values from 0.1 to 1.9
- mlp_up: bfloat16 [2048, 512], P(('lat', 'lon')), may hold values from -0.25 to 0.25
- mlp_down: bfloat16 [2048, 512], P(('lat', 'lon')), may hold values from -0.125 to 0.125
Outputs:
- latents_out: bfloat16 [3, 96, 384, 512], P(None, 'lat', 'lon')
Inputs may be any that keep to these rules, and one draw needn't show every extreme that they name: `enc_scale`: one logit scale for each head. `swin_scale`: one logit scale for each head.
All inputs are finite; a program needn't handle non-finite values.
Results may differ from a plain program's by a relative error of at most 0.018.
The roundings to bfloat16 on the way count: a program that leaves them out, or rounds other values in their place, can miss the bound.
Values may be sent and summed in bfloat16 or wider, within the bound.
No kernel may reach another device: no remote copies, remote signals or barrier semaphores. Data moves between devices by JAX's collectives and lax.ppermute only.
A program may use at most 128 MiB of HBM per device.

v0:
```python
import math

import jax
import jax.numpy as jnp
from jax import lax
from jax.sharding import PartitionSpec as P

WH = 6
WW = 12


epsilon = 1e-05
masked_score = -1e30


def extended(shard, sides, width, wrap):
    for axis, dim in sides:
        size, length = (lax.axis_size(axis), shard.shape[dim])
        up = [(i, (i + 1) % size) for i in range(size if wrap else size - 1)]
        down = [(j, i) for i, j in up]
        last = lax.slice_in_dim(shard, length - width, length, axis=dim)
        first = lax.slice_in_dim(shard, 0, width, axis=dim)
        before = lax.ppermute(last, axis, up)
        after = lax.ppermute(first, axis, down)
        shard = jnp.concatenate([before, shard, after], axis=dim)
    return shard


def layer_norm(values, gain_vector):
    average = jnp.mean(values, axis=-1, keepdims=True)
    centred = values - average
    spread = jnp.mean(centred * centred, axis=-1, keepdims=True)
    return centred * lax.rsqrt(spread + epsilon) * gain_vector


def encode_levels(
    patches, patch_weight, level_embed, enc_gain, latent_query, kv_weight, enc_scale, enc_out_weight
):
    level_count, patch_count, channels = patches.shape
    model_width = patch_weight.shape[1]
    head_count = enc_scale.shape[0]
    head_size = model_width // head_count
    embedded = jnp.dot(
        patches.reshape(level_count * patch_count, channels),
        patch_weight,
        preferred_element_type=jnp.float32,
    )
    embedded = embedded.reshape(level_count, patch_count, model_width) + level_embed[:, None, :]
    level_tokens = layer_norm(embedded, enc_gain).astype(jnp.bfloat16)
    keyval = jnp.dot(
        level_tokens.reshape(level_count * patch_count, model_width),
        kv_weight,
        preferred_element_type=jnp.float32,
    ).astype(jnp.bfloat16)
    keyval = keyval.reshape(level_count, patch_count, 2, head_count, head_size)
    queries = latent_query.reshape(-1, head_count, head_size)
    level_scores = jnp.einsum(
        "lhd,kphd->klhp", queries, keyval[:, :, 0], preferred_element_type=jnp.float32
    )
    level_scores = level_scores * (enc_scale / math.sqrt(head_size))[None, None, :, None]
    highest = jnp.max(level_scores, axis=0, keepdims=True)
    raised = jnp.exp(level_scores - highest)
    level_weights = (raised / jnp.sum(raised, axis=0, keepdims=True)).astype(jnp.bfloat16)
    pooled = jnp.einsum(
        "klhp,kphd->plhd", level_weights, keyval[:, :, 1], preferred_element_type=jnp.float32
    ).astype(jnp.bfloat16)
    latent_count = queries.shape[0]
    encoded = jnp.dot(
        pooled.reshape(patch_count * latent_count, model_width),
        enc_out_weight,
        preferred_element_type=jnp.float32,
    )
    return (
        encoded.reshape(patch_count, latent_count, model_width)
        + latent_query.astype(jnp.float32)[None]
    )


def attend_windows(block_in, row_valid, attn_gain, qkv_weight, swin_scale):
    latent_count, row_count, col_count, model_width = block_in.shape
    head_count = swin_scale.shape[0]
    head_size = model_width // head_count
    row_windows = row_count // WH
    col_windows = col_count // WW
    window_size = latent_count * WH * WW
    normed = layer_norm(block_in.astype(jnp.float32), attn_gain).astype(jnp.bfloat16)
    projected = jnp.dot(
        normed.reshape(-1, model_width), qkv_weight, preferred_element_type=jnp.float32
    ).astype(jnp.bfloat16)
    projected = projected.reshape(
        latent_count, row_windows, WH, col_windows, WW, 3, head_count, head_size
    )
    projected = projected.transpose(1, 3, 0, 2, 4, 5, 6, 7).reshape(
        row_windows * col_windows, window_size, 3, head_count, head_size
    )
    queries = projected[:, :, 0]
    key_part = projected[:, :, 1]
    value_part = projected[:, :, 2]
    window_scores = jnp.einsum(
        "wqhd,wkhd->whqk", queries, key_part, preferred_element_type=jnp.float32
    )
    window_scores = window_scores * (swin_scale / math.sqrt(head_size))[None, :, None, None]
    key_valid = jnp.broadcast_to(
        row_valid.reshape(1, row_windows, WH, 1, 1),
        (latent_count, row_windows, WH, col_windows, WW),
    )
    key_valid = key_valid.transpose(1, 3, 0, 2, 4).reshape(
        row_windows * col_windows, 1, 1, window_size
    )
    window_scores = jnp.where(key_valid, window_scores, masked_score)
    highest = jnp.max(window_scores, axis=-1, keepdims=True)
    raised = jnp.exp(window_scores - highest)
    window_weights = (raised / jnp.sum(raised, axis=-1, keepdims=True)).astype(jnp.bfloat16)
    window_mixed = jnp.einsum(
        "whqk,wkhd->wqhd", window_weights, value_part, preferred_element_type=jnp.float32
    ).astype(jnp.bfloat16)
    window_mixed = window_mixed.reshape(row_windows, col_windows, latent_count, WH, WW, model_width)
    return window_mixed.transpose(2, 0, 3, 1, 4, 5).reshape(
        latent_count, row_count, col_count, model_width
    )


def project(window_mixed, proj_weight):
    shape_in = window_mixed.shape
    flat_rows = jnp.dot(
        window_mixed.reshape(-1, shape_in[-1]), proj_weight, preferred_element_type=jnp.float32
    )
    return flat_rows.astype(jnp.bfloat16).reshape(shape_in)


def grow_with(source, pieces):
    hidden = lax.dot_general(
        source, pieces[0], (((1,), (1,)), ((), ())), preferred_element_type=jnp.float32
    )
    hidden = jax.nn.gelu(hidden, approximate=False).astype(jnp.bfloat16)
    return jnp.dot(hidden, pieces[1], preferred_element_type=jnp.float32)


def shards(
    fields,
    surface_kind,
    patch_weight,
    level_embed,
    enc_gain,
    latent_query,
    kv_weight,
    enc_scale,
    enc_out_weight,
    kind_embed,
    attn_gain,
    qkv_weight,
    swin_scale,
    proj_weight,
    mlp_gain,
    mlp_up,
    mlp_down,
):
    by_rows = lax.all_to_all(fields, "lat", split_axis=1, concat_axis=0, tiled=True)
    level_count, row_count, flat_width = by_rows.shape
    channels, model_width = patch_weight.shape
    col_count = flat_width // channels
    patches = by_rows.reshape(level_count, row_count * col_count, channels)
    encoded = encode_levels(
        patches,
        patch_weight,
        level_embed,
        enc_gain,
        latent_query,
        kv_weight,
        enc_scale,
        enc_out_weight,
    )
    kind_ids = surface_kind.reshape(-1)
    kind_add = jnp.zeros((row_count * col_count, model_width), jnp.float32)
    for kind_id in range(kind_embed.shape[0]):
        kind_add = kind_add + jnp.where(
            (kind_ids == kind_id)[:, None], kind_embed[kind_id][None, :], 0.0
        )
    latent_count = latent_query.shape[0]
    latents = (encoded + kind_add[:, None, :]).astype(jnp.bfloat16)
    latents = latents.reshape(row_count, col_count, latent_count, model_width).transpose(2, 0, 1, 3)
    half_rows = WH // 2
    half_cols = WW // 2
    tall_block = extended(latents, (("lat", 1),), half_rows, False)
    global_row = (
        lax.axis_index("lat") * row_count
        - half_rows
        + jnp.arange(row_count + 2 * half_rows, dtype=jnp.int32)
    )
    row_valid = (global_row >= 0) & (global_row < row_count * lax.axis_size("lat"))
    wide_block = extended(tall_block, (("lon", 2),), half_cols, True)
    window_mixed = attend_windows(wide_block, row_valid, attn_gain, qkv_weight, swin_scale)
    kept_rows = window_mixed[
        :, half_rows : half_rows + row_count, half_cols : half_cols + col_count
    ]
    attended = project(kept_rows, proj_weight)
    residual = latents.astype(jnp.float32) + attended.astype(jnp.float32)
    flat_resid = residual.reshape(-1, model_width)
    tokens = layer_norm(flat_resid, mlp_gain).astype(jnp.bfloat16)
    summed = grow_with(
        tokens,
        (
            lax.all_gather(mlp_up, ("lat", "lon"), axis=0, tiled=True),
            lax.all_gather(mlp_down, ("lat", "lon"), axis=0, tiled=True),
        ),
    )
    output = (flat_resid + summed).astype(jnp.bfloat16)
    return output.reshape(latents.shape)


def solution(mesh):
    return jax.shard_map(
        shards,
        mesh=mesh,
        in_specs=(
            P("lat", None, "lon"),
            P("lat", "lon"),
            P(),
            P(),
            P(),
            P(),
            P(),
            P(),
            P(),
            P(),
            P(),
            P(),
            P(),
            P(),
            P(),
            P(("lat", "lon"), None),
            P(("lat", "lon"), None),
        ),
        out_specs=P(None, "lat", "lon", None),
        check_vma=False,
    )
```

profile of v0, /device:TPU:1, one launch (start us, length us, event | category | flops | bytes accessed | tf_op | source)
XLA Modules:
  0.0 656.3 jit_solution(13625568466367348688)
XLA Ops:
  9.1 6.0 all-to-all-start
  21.1 6.2 all-to-all-done
  32.9 5.9 convolution_convert_fusion.1
  38.8 10.1 %copy.48 = bf16[3456,1024]{0,1:T(8,128)(2,1)} copy(bf16[3456,1024]{1,0:T(8,128)(2,1)} %convolution_convert_fusion.1) | data formatting | bytes 14155776 | tf_op jit(solution)/shard_map/convert_element_type | solution.py:54
  48.8 20.6 %reshape.239 = bf16[12,288,2,8,64]{1,0,4,3,2:T(8,128)(2,1)} reshape(bf16[3456,1024]{0,1:T(8,128)(2,1)} %copy.48) | data formatting | bytes 14155776 | tf_op jit(solution)/shard_map/reshape | solution.py:55
  69.4 9.2 %fusion.97 = (bf16[12,288,1,8,64]{1,0,4,3,2:T(8,128)(2,1)}, bf16[12,288,1,8,64]{1,0,4,3,2:T(8,128)(2,1)S(1)}) fusion(bf16[12,288,2,8,64]{1,0,4,3,2:T(8,128)(2,1)} %reshape.239), kind=kLoop, calls=%fused_computation.125 | loop fusion | bytes 14155776 | tf_op jit(solution)/shard_map/slice | solution.py:65
  79.9 3.0 copy.52
  82.8 21.8 %copy.76 = bf16[12,288,1,8,64]{4,0,3,1,2:T(8,128)(2,1)} copy(bf16[12,288,1,8,64]{1,0,4,3,2:T(8,128)(2,1)} %get-tuple-element.10) | data formatting | bytes 7077888
  104.6 8.5 %convert_bitcast_fusion.1 = bf16[288,3,8,64]{3,1,2,0:T(4,128)(2,1)} fusion(bf16[12,3,8,288]{0,1,2,3:T(4,128)(2,1)} %copy.52, bf16[12,288,1,8,64]{4,0,3,1,2:T(8,128)(2,1)} %copy.76), kind=kOutput, calls=%fused_computation.53 | convolution fusion | flops 11059200 | bytes 4589568 | tf_op jit(solution)/shard_map/klhp,kphd->plhd/dot_general | solution.py:64
  113.1 3.2 copy.53
  125.5 6.0 collective-permute-done.1
  134.3 5.0 collective-permute-start.3
  140.1 7.3 %collective-permute-done.2 = bf16[3,30,6,512]{3,1,2,0:T(8,128)(2,1)} collective-permute-done((bf16[3,30,6,512]{3,1,2,0:T(8,128)(2,1)S(1)}, bf16[3,30,6,512]{3,1,2,0:T(8,128)(2,1)}, u32[]{:S(2)}, u32[]{:S(2)}) %collective-permute-start.2) | collective-permute-done | bytes 552992 | tf_op jit(solution)/shard_map/ppermute | solution.py:23
  153.4 3.9 multiply_reduce_fusion.1
  161.9 5.5 convolution_convert_fusion
  167.4 17.0 %reshape.242 = bf16[3,5,6,2,12,3,8,64]{7,6,5,4,3,2,1,0:T(8,128)(2,1)} reshape(bf16[2160,1536]{1,0:T(8,128)(2,1)} %convolution_convert_fusion) | data formatting | bytes 13271040 | tf_op jit(solution)/shard_map/reshape | solution.py:90
  184.3 7.2 %copy.62 = bf16[3,5,6,2,12,3,8,64]{7,6,5,4,2,0,3,1:T(8,128)(2,1)S(1)} copy(bf16[3,5,6,2,12,3,8,64]{7,6,5,4,3,2,1,0:T(8,128)(2,1)} %reshape.242) | data formatting | bytes 13271040 | tf_op jit(solution)/shard_map/reshape | solution.py:90
  191.5 5.3 fusion.96
  196.8 6.0 copy.79
  202.8 6.1 copy.80
  208.9 6.1 copy.78
  215.0 12.1 %fusion.102 = (f32[10,8,216]{2,1,0:T(8,128)S(1)}, f32[10,8,216,216]{2,3,1,0:T(8,128)}) fusion(f32[8]{0:T(128)S(1)} %copy-done.15, pred[10,216]{1,0:T(8,128)(4,1)S(1)} %broadcast_in_dim.96, bf16[10,216,1,8,64]{1,4,3,0,2:T(8,128)(2,1)} %copy.80, bf16[10,216,1,8,64]{1,4,3,0,2:T(8,128)(2,1)} %copy.79), kind=kOutput, calls=%fused_computation.130 | convolution fusion | flops 492687584 | bytes 19424912 | tf_op jit(solution)/shard_map/sub | solution.py:112
  227.1 10.3 %convert_bitcast_fusion = bf16[10,216,8,64]{1,3,2,0:T(8,128)(2,1)} fusion(f32[10,8,216,216]{2,3,1,0:T(8,128)} %get-tuple-element.27, f32[10,8,216]{2,1,0:T(8,128)S(1)} %get-tuple-element.26, bf16[10,216,1,8,64]{1,4,3,0,2:T(8,128)(2,1)} %copy.78), kind=kOutput, calls=%fused_computation.50 | convolution fusion | flops 486328320 | bytes 19422720 | tf_op jit(solution)/shard_map/whqk,wkhd->wqhd/dot_general | solution.py:114
  237.4 6.9 %copy.67 = bf16[10,216,8,64]{3,2,0,1:T(8,128)(2,1)} copy(bf16[10,216,8,64]{1,3,2,0:T(8,128)(2,1)} %convert_bitcast_fusion) | data formatting | bytes 4423680 | tf_op jit(solution)/shard_map/convert_element_type | solution.py:116
  244.3 7.6 %reshape.244 = bf16[5,2,3,6,12,512]{5,1,0,4,3,2:T(2,128)(2,1)} reshape(bf16[10,216,8,64]{3,2,0,1:T(8,128)(2,1)} %copy.67) | data formatting | bytes 4423680 | tf_op jit(solution)/shard_map/reshape | solution.py:117
  252.0 4.0 copy.68
  256.0 4.9 reshape.245
  263.9 3.0 fusion.46
  269.6 3.4 fusion.95
  277.1 44.2 %all-gather.3.cloned.1.call-done = bf16[2048,512]{1,0:T(8,128)(2,1)} async-done(((bf16[16,512]{1,0:T(8,128)(2,1)}), bf16[2048,512]{1,0:T(8,128)(2,1)}) %all-gather.3.cloned.1.call-update) | async-done | bytes 2097168 | tf_op jit(solution)/shard_map/all_gather | solution.py:203
  321.3 305.0 %all-gather.5.cloned.1.call-done = bf16[2048,512]{1,0:T(8,128)(2,1)} async-done(((bf16[16,512]{1,0:T(8,128)(2,1)}), bf16[2048,512]{1,0:T(8,128)(2,1)}) %all-gather.5.cloned.1.call-update) | async-done | bytes 2097168 | tf_op jit(solution)/shard_map/all_gather | solution.py:204
  626.3 20.3 %add_convert_fusion = bf16[864,512]{1,0:T(8,128)(2,1)} fusion(f32[864,512]{1,0:T(8,128)S(1)} %reshape.247, bf16[2048,512]{1,0:T(8,128)(2,1)} %all-gather.5.cloned.1.call-done, bf16[2048,512]{1,0:T(8,128)(2,1)} %all-gather.3.cloned.1.call-done, f32[512]{0:T(512)S(1)} %copy-done.13, f32[864]{0:T(1024)S(1)} %rsqrt.34, f32[864]{0:T(1024)S(1)} %div.56), kind=kOutput, calls=%fused_computation.56 | convolution fusion | flops 3741548544 | bytes 6857472 | tf_op jit(solution)/shard_map/dot_general | solution.py:136
  (95 shorter events, 51.0 us)
Async XLA Ops:
  6.5 155.3 %copy-start = (bf16[512,1536]{1,0:T(8,128)(2,1)S(1)}, bf16[512,1536]{1,0:T(8,128)(2,1)}, u32[]{:S(2)}) copy-start(bf16[512,1536]{1,0:T(8,128)(2,1)} %param.28) | copy-start | bytes 4718596
  6.5 21.9 %copy-start.8 = (bf16[80,512]{1,0:T(8,128)(2,1)S(1)}, bf16[80,512]{1,0:T(8,128)(2,1)}, u32[]{:S(2)}) copy-start(bf16[80,512]{1,0:T(8,128)(2,1)} %param.19) | copy-start | bytes 245764
  6.5 21.9 %copy-start.7 = (f32[12,512]{1,0:T(8,128)S(1)}, f32[12,512]{1,0:T(8,128)}, u32[]{:S(2)}) copy-start(f32[12,512]{1,0:T(8,128)} %param.20) | copy-start | bytes 73732
  9.1 18.3 %all-to-all-start = ((bf16[3,96,960]{2,0,1:T(4,128)(2,1)}), bf16[3,96,960]{2,0,1:T(4,128)(2,1)S(1)}, u32[]{:S(2)}, u32[]{:S(2)}) async-start(bf16[3,96,960]{2,0,1:T(4,128)(2,1)} %copy.45), calls=%async_computation | async-start | bytes 1572864 | tf_op jit(solution)/shard_map/all_to_all | solution.py:158
  15.1 306.2 %all-gather.3.cloned.1.call-start = ((), (), s32[]{:S(2)}) async-start(), calls=%async_computation.1 | async-start | bytes 2113536 | tf_op jit(solution)/shard_map/all_gather | solution.py:203
  15.8 610.5 %all-gather.5.cloned.1.call-start = ((), (), s32[]{:S(2)}) async-start(), calls=%async_computation.2 | async-start | bytes 2113536 | tf_op jit(solution)/shard_map/all_gather | solution.py:204
  29.7 1.8 copy-start.10
  31.5 1.3 copy-start.12
  104.6 11.7 %copy-start.5 = (f32[288,512]{1,0:T(8,128)S(1)}, f32[288,512]{1,0:T(8,128)}, u32[]{:S(2)}) copy-start(f32[288,512]{1,0:T(8,128)} %select_add_fusion) | copy-start | bytes 1769476
  120.6 18.9 %copy-start.14 = (f32[8]{0:T(128)S(1)}, f32[8]{0:T(128)}, u32[]{:S(2)}) copy-start(f32[8]{0:T(128)} %param.29) | copy-start | bytes 100
  120.6 4.8 collective-permute-start
  123.4 8.1 %collective-permute-start.1 = (bf16[3,3,12,512]{3,2,1,0:T(8,128)(2,1)S(1)}, bf16[3,3,12,512]{3,2,1,0:T(8,128)(2,1)S(1)}, u32[]{:S(2)}, u32[]{:S(2)}) collective-permute-start(bf16[3,3,12,512]{3,2,1,0:T(8,128)(2,1)S(1)} %get-tuple-element.15), channel_id=1, source_target_pairs={{32,0},{64,32},{96,64},{33,1},{65,33},{97,65},{34,2},{66,34},{98,6... | collective-permute-start | bytes 331784 | tf_op jit(solution)/shard_map/ppermute | solution.py:24
  125.5 8.8 %copy-start.3 = (bf16[3,3,12,512]{3,2,1,0:T(8,128)(2,1)}, bf16[3,3,12,512]{3,2,1,0:T(8,128)(2,1)S(1)}, u32[]{:S(2)}) copy-start(bf16[3,3,12,512]{3,2,1,0:T(8,128)(2,1)S(1)} %collective-permute-done) | copy-start | bytes 331780
  131.5 2.8 copy-start.4
  132.2 15.2 %collective-permute-start.2 = (bf16[3,30,6,512]{3,1,2,0:T(8,128)(2,1)S(1)}, bf16[3,30,6,512]{3,1,2,0:T(8,128)(2,1)}, u32[]{:S(2)}, u32[]{:S(2)}) collective-permute-start(bf16[3,30,6,512]{3,1,2,0:T(8,128)(2,1)S(1)} %copy.58), channel_id=1, source_target_pairs={{0,1},{1,2},{2,3},{3,4},{4,5},{5,6},{6,7},{7,8},{8,9},{9,10},{10,1... | collective-permute-start | bytes 1658888 | tf_op jit(solution)/shard_map/ppermute | solution.py:23
  134.3 14.4 %collective-permute-start.3 = (bf16[3,30,6,512]{3,1,2,0:T(8,128)(2,1)}, bf16[3,30,6,512]{3,1,2,0:T(8,128)(2,1)}, u32[]{:S(2)}, u32[]{:S(2)}) collective-permute-start(bf16[3,30,6,512]{3,1,2,0:T(8,128)(2,1)} %copy.59), channel_id=1, source_target_pairs={{1,0},{2,1},{3,2},{4,3},{5,4},{6,5},{7,6},{8,7},{9,8},{10,9},{11,1... | collective-permute-start | bytes 1658888 | tf_op jit(solution)/shard_map/ppermute | solution.py:24
  150.2 0.9 copy-start.2
  158.1 2.5 copy-start.9
  158.1 2.5 copy-start.11
  208.9 6.1 copy-start.15
  255.9 8.0 %copy-start.6 = (bf16[512,512]{1,0:T(8,128)(2,1)S(1)}, bf16[512,512]{1,0:T(8,128)(2,1)}, u32[]{:S(2)}) copy-start(bf16[512,512]{1,0:T(8,128)(2,1)} %param.30) | copy-start | bytes 1572868
  273.0 353.3 %copy-start.13 = (f32[512]{0:T(512)S(1)}, f32[512]{0:T(512)}, u32[]{:S(2)}) copy-start(f32[512]{0:T(512)} %param.31) | copy-start | bytes 6148
  626.3 23.0 %copy-start.1 = (bf16[512,1536]{1,0:T(8,128)(2,1)S(1)}, bf16[512,1536]{1,0:T(8,128)(2,1)}, u32[]{:S(2)}) copy-start(bf16[512,1536]{1,0:T(8,128)(2,1)} %param.28) | copy-start | bytes 4718596
Sparse Core Ops, SparseCore 0:
  17.6 303.6 all-gather.2
  323.0 303.3 all-gather.4
where the time goes:
time: 662 us; the launch traced here: 656 us
  waiting for transfers between devices  370 us (56%)
  local copies, waits for them, and re-layouts  163 us (25%)
  matrix products  70.3 us (11%)
  other arithmetic  22.8 us (3%)
  starting transfers between devices  16.8 us (3%)
  between operations  14 us (2%)
    all_gather x1, waiting for transfers between devices, shards(): lax.all_gather(mlp_down, ('lat', 'lon'), axis=0, tiled=True)  305 us
    all_gather x1, waiting for transfers between devices, shards(): lax.all_gather(mlp_up, ('lat', 'lon'), axis=0, tiled=True)  44.2 us
    unnamed x37, local copies, waits for them, and re-layouts  43.4 us
    reshape x2, local copies, waits for them, and re-layouts, attend_windows(): projected.reshape(latent_count, row_windows, WH, col_windows, WW, 3, head...  24.1 us
    reshape x1, local copies, waits for them, and re-layouts, encode_levels(): keyval = keyval.reshape(level_count, patch_count, 2, head_count, head_size)  20.6 us
    dot_general x1, matrix products, grow_with(): return jnp.dot(hidden, pieces[1], preferred_element_type=jnp.float32)  20.3 us
  transfers between devices with their start and end apart: 7, of which 6 were waited for; matrix products, arithmetic and copies ran while one was open for 35% of the time, Pallas kernels for 0%

commit v1 on v0

v1 whole, which is shorter than its diff:
```python
import functools
import math

import jax
import jax.numpy as jnp
from jax import lax
from jax.experimental import pallas as pl
from jax.experimental.pallas import tpu as pltpu
from jax.sharding import PartitionSpec as P

WH = 6
WW = 12
HALF = WW // 2
SHIFT = WH // 2
LEVELS_EACH = 3
LATENT = 3
HEADS = 8
HEAD = 64
CHAN = 80
D = 512
ROWS = 24
SPAN = HALF * CHAN
WINDOWS = ROWS // WH
GROUP = WH * LATENT * HALF
PADDED = 112
STEP = LATENT * HALF
EDGE = 64

epsilon = 1e-05
masked_score = -1e30
f32 = jnp.float32
bf16 = jnp.bfloat16

VMEM = pl.BlockSpec(memory_space=pltpu.VMEM)
SMEM = pl.BlockSpec(memory_space=pltpu.SMEM)


def dot(a, b):
    return jnp.dot(a, b, preferred_element_type=f32)


def dot_nt(a, b):
    return lax.dot_general(a, b, (((1,), (1,)), ((), ())), preferred_element_type=f32)


def layer_norm(values, gain_vector):
    average = jnp.mean(values, axis=-1, keepdims=True)
    centred = values - average
    spread = jnp.mean(centred * centred, axis=-1, keepdims=True)
    return centred * lax.rsqrt(spread + epsilon) * gain_vector


def pack_kernel(place, fields, kind, *rest):
    outs, (left, right) = rest[:8], rest[8:]
    kinds = kind[...].astype(f32)
    kinds = jnp.concatenate([kinds[ROWS - SHIFT :], kinds[: ROWS - SHIFT]], axis=0)
    left[:, :, SPAN:] = jnp.zeros((4, 3 * ROWS, D - SPAN), f32)
    right[:, :, SPAN:] = jnp.zeros((4, 3 * ROWS, D - SPAN), f32)
    for level in range(LEVELS_EACH):
        part = fields[level].astype(f32)
        count = part.shape[0]
        part = jnp.concatenate([part[count - SHIFT :], part[: count - SHIFT]], axis=0)
        for to in range(4):
            rows = part[to * ROWS : (to + 1) * ROWS]
            left[to, level * ROWS : (level + 1) * ROWS, :SPAN] = rows[:, :SPAN]
            right[to, level * ROWS : (level + 1) * ROWS, :SPAN] = rows[:, SPAN:]
    for to in range(4):
        left[to, :ROWS, SPAN : SPAN + HALF] = kinds[:, :HALF]
        right[to, :ROWS, SPAN : SPAN + HALF] = kinds[:, HALF:]
    for step in range(4):
        to = lax.rem(place[0] + step, 4)
        outs[step][...] = left[to].astype(bf16)
        outs[4 + step][...] = right[to].astype(bf16)


def encode_kernel(
    place,
    enc_scale,
    piece0,
    piece1,
    piece2,
    piece3,
    patch_weight,
    level_embed,
    enc_gain,
    latent_query,
    kv_weight,
    enc_out_weight,
    kind_embed,
    out,
    shifted,
    spread,
    *,
    chunk,
):
    lat = place[0]
    pieces = [piece[...].astype(f32) for piece in (piece0, piece1, piece2, piece3)]
    row_at = lax.broadcasted_iota(jnp.int32, (ROWS, D - SPAN), 0)
    kinds = jnp.where(row_at < SHIFT, pieces[1][:ROWS, SPAN:], pieces[0][:ROWS, SPAN:])
    patches = jnp.concatenate(pieces, axis=0).astype(bf16)
    embeds = []
    for step in range(4):
        start = lax.rem(lat - step + 4, 4) * LEVELS_EACH
        for level in range(LEVELS_EACH):
            embeds.append(
                jnp.broadcast_to(level_embed[pl.ds(start + level, 1), :], (ROWS, D))
            )
    embeds = jnp.concatenate(embeds, axis=0)
    gain = enc_gain[...]
    shifted[...] = jnp.zeros(shifted.shape, bf16)
    for col in range(HALF):
        offset = col * CHAN % 128
        shifted[col, offset : offset + CHAN, :] = patch_weight[...]
    queries = latent_query[...].astype(f32)
    head_at = lax.broadcasted_iota(jnp.int32, (HEADS, D), 0)
    lane_at = lax.broadcasted_iota(jnp.int32, (HEADS, D), 1) // HEAD
    in_head = jnp.where(head_at == lane_at, 1.0, 0.0).astype(f32)
    query_rows = jnp.concatenate(
        [in_head * queries[latent : latent + 1] for latent in range(LATENT)], axis=0
    ).astype(bf16)
    nothing = jnp.zeros((HEADS, D), f32)
    widen = [
        jnp.concatenate(
            [in_head if at == latent else nothing for at in range(LATENT)], axis=0
        ).astype(bf16)
        for latent in range(LATENT)
    ]
    lane = lax.broadcasted_iota(jnp.int32, (1, LATENT * HEADS), 1) % HEADS
    scale = jnp.zeros((1, LATENT * HEADS), f32)
    for head in range(HEADS):
        scale = jnp.where(lane == head, enc_scale[head] / math.sqrt(HEAD), scale)
    count = patches.shape[0]
    levels = count // ROWS
    for first in range(0, HALF, chunk):
        tokens = []
        for col in range(first, first + chunk):
            base = col * CHAN // 128 * 128
            depth = min(192, D - base)
            embedded = dot(patches[:, base : base + depth], shifted[col, :depth, :]) + embeds
            tokens.append(layer_norm(embedded, gain).astype(bf16))
        tokens = jnp.concatenate(tokens, axis=0)
        keys = dot(tokens, kv_weight[:, :D]).astype(bf16)
        values = dot(tokens, kv_weight[:, D:]).astype(bf16).astype(f32)
        scores = dot_nt(keys, query_rows) * scale
        scores = scores.reshape(chunk, levels, ROWS, LATENT * HEADS)
        highest = jnp.max(scores, axis=1, keepdims=True)
        raised = jnp.exp(scores - highest)
        weights = raised / jnp.sum(raised, axis=1, keepdims=True)
        weights = weights.reshape(chunk * count, LATENT * HEADS).astype(bf16)
        pooled = []
        for latent in range(LATENT):
            wide = dot(weights, widen[latent]) * values
            pooled.append(jnp.sum(wide.reshape(chunk, levels, ROWS, D), axis=1))
        pooled = jnp.concatenate(
            [pooled[latent][at] for at in range(chunk) for latent in range(LATENT)], axis=0
        ).astype(bf16)
        encoded = dot(pooled, enc_out_weight[...])
        for at in range(chunk):
            col = first + at
            kind = kinds[:, col : col + 1]
            kind_add = jnp.where(
                kind < 0.5,
                kind_embed[0:1, :],
                jnp.where(kind < 1.5, kind_embed[1:2, :], kind_embed[2:3, :]),
            )
            for latent in range(LATENT):
                start = (at * LATENT + latent) * ROWS
                value = encoded[start : start + ROWS] + queries[latent : latent + 1] + kind_add
                value = value.astype(bf16).astype(f32)
                for tile in range(D // 128):
                    spread[tile, pl.ds(latent * HALF + col, ROWS, stride=STEP), :] = value[
                        :, tile * 128 : (tile + 1) * 128
                    ]
    for tile in range(D // 128):
        spread[tile, WINDOWS * GROUP :, :] = jnp.zeros((8, 128), f32)
        for window in range(WINDOWS):
            out[window * PADDED : (window + 1) * PADDED, tile * 128 : (tile + 1) * 128] = spread[
                tile, pl.ds(window * GROUP, PADDED), :
            ].astype(bf16)


def window_kernel(
    place,
    swin_scale,
    block0,
    block1,
    attn_gain,
    qkv_weight,
    proj_weight,
    resid0,
    resid1,
    qkv0,
    qkv1,
    mixed0,
    mixed1,
):
    gain = attn_gain[...]
    for block, qkv in ((block0, qkv0), (block1, qkv1)):
        normed = layer_norm(block[...].astype(f32), gain).astype(bf16)
        qkv[...] = dot(normed, qkv_weight[...]).astype(bf16)
    size = 2 * PADDED
    key_at = lax.broadcasted_iota(jnp.int32, (size, size), 1)
    key_at = jnp.where(key_at >= PADDED, key_at - PADDED, key_at)
    query_at = lax.broadcasted_iota(jnp.int32, (size, size), 0)
    query_at = jnp.where(query_at >= PADDED, query_at - PADDED, query_at)
    off = jnp.where(key_at < GROUP, 0.0, masked_score).astype(f32)
    apart = jnp.where((key_at < GROUP // 2) != (query_at < GROUP // 2), masked_score, 0.0)
    first_off = off + apart * jnp.where(place[0] == 0, 1.0, 0.0).astype(f32)
    off_row = off[0:1]
    lane = lax.broadcasted_iota(jnp.int32, (1, 128), 1)
    low = lane < HEAD
    sides = [jnp.where(low, 1.0, 0.0).astype(bf16), jnp.where(low, 0.0, 1.0).astype(bf16)]
    for window in range(WINDOWS):
        rows = slice(window * PADDED, (window + 1) * PADDED)
        bias = first_off if window == 0 else off_row
        for pair in range(HEADS // 2):
            query, key, value = [
                jnp.concatenate(
                    [
                        qkv[rows, part * D + pair * 128 : part * D + (pair + 1) * 128]
                        for qkv in (qkv0, qkv1)
                    ],
                    axis=0,
                )
                for part in range(3)
            ]
            sums = []
            for side in range(2):
                scores = dot_nt(query * sides[side], key) + bias
                highest = jnp.max(scores, axis=-1, keepdims=True)
                factor = swin_scale[2 * pair + side] * (math.log2(math.e) / math.sqrt(HEAD))
                raised = jnp.exp2((scores - highest) * factor)
                total = jnp.sum(raised, axis=-1, keepdims=True)
                weights = (raised * (1.0 / total)).astype(bf16)
                sums.append(dot(weights, value))
            both = jnp.where(low, sums[0], sums[1]).astype(bf16)
            mixed0[rows, pair * 128 : (pair + 1) * 128] = both[:PADDED]
            mixed1[rows, pair * 128 : (pair + 1) * 128] = both[PADDED:]
    for block, mixed, resid in ((block0, mixed0, resid0), (block1, mixed1, resid1)):
        attended = dot(mixed[...], proj_weight[...]).astype(bf16).astype(f32)
        resid[...] = block[...].astype(f32) + attended


def feed_kernel(resid, mlp_gain, mine, other, out, edge):
    values = resid[...]
    tokens = layer_norm(values, mlp_gain[...]).astype(bf16)
    total = values
    for weights in (mine, other):
        count = weights.shape[0]
        for start in range(0, count, 512):
            up = weights[start : start + 512, :D]
            down = weights[start : start + 512, D:]
            hidden = dot_nt(tokens, up)
            hidden = hidden * (1.0 + lax.erf(hidden * math.sqrt(0.5))) * 0.5
            total = total + dot(hidden.astype(bf16), down)
    total = total.astype(bf16)
    out[...] = total
    edge[...] = total[:EDGE]


def join_kernel(own, own_edge, far, far_edge, out, low, high):
    for source, tail, held in ((own, own_edge, low), (far, far_edge, high)):
        part = source[...].astype(f32)
        for window in range(WINDOWS):
            held[window * GROUP : (window + 1) * GROUP, :] = part[
                window * PADDED : window * PADDED + GROUP
            ]
        held[WINDOWS * GROUP : WINDOWS * GROUP + GROUP // 2, :] = tail[...].astype(f32)[
            : GROUP // 2
        ]
    for row in range(ROWS):
        for latent in range(LATENT):
            start = (row + SHIFT) * STEP + latent * HALF
            pair = jnp.concatenate(
                [low[start : start + HALF, :], high[start : start + HALF, :]], axis=0
            )
            out[latent, row] = pair.astype(bf16)


def params():
    return pltpu.CompilerParams(vmem_limit_bytes=56 * 1024 * 1024)


def struct(shape, dtype):
    return jax.ShapeDtypeStruct(shape, dtype)


def gather_weights(mlp_up, mlp_down, lon_count):
    held = jnp.concatenate([mlp_up, mlp_down], axis=1)
    for bits in (3, 12):
        unit = bits // 3
        moved = [
            lax.ppermute(
                held,
                "lon",
                [(i, (i & ~bits) | ((i + step * unit) & bits)) for i in range(lon_count)],
            )
            for step in (1, 2, 3)
        ]
        held = jnp.concatenate([held] + moved, axis=0)
    moved = [
        lax.ppermute(
            held,
            ("lat", "lon"),
            [
                (a * lon_count + b, ((a + 2 * far) % 4) * lon_count + (b ^ (16 * near)))
                for a in range(4)
                for b in range(lon_count)
            ],
        )
        for far, near in ((0, 1), (1, 0), (1, 1))
    ]
    mine = jnp.concatenate([held] + moved, axis=0)
    other = lax.ppermute(mine, "lat", [(a, a ^ 1) for a in range(4)])
    return mine, other


def move(array, lat_step, lon_step, lon_count):
    perm = [
        (a * lon_count + b, ((a + lat_step) % 4) * lon_count + (b + lon_step) % lon_count)
        for a in range(4)
        for b in range(lon_count)
    ]
    return lax.ppermute(array, ("lat", "lon"), perm)


def shards(
    lon_count,
    fields,
    surface_kind,
    patch_weight,
    level_embed,
    enc_gain,
    latent_query,
    kv_weight,
    enc_scale,
    enc_out_weight,
    kind_embed,
    attn_gain,
    qkv_weight,
    swin_scale,
    proj_weight,
    mlp_gain,
    mlp_up,
    mlp_down,
):
    place = lax.axis_index("lat").astype(jnp.int32).reshape(1)
    piece = struct((LEVELS_EACH * ROWS, D), bf16)
    packed = pl.pallas_call(
        pack_kernel,
        out_shape=[piece] * 8,
        in_specs=[SMEM, VMEM, VMEM],
        out_specs=[VMEM] * 8,
        scratch_shapes=[pltpu.VMEM((4, LEVELS_EACH * ROWS, D), f32)] * 2,
        compiler_params=params(),
        name="pack",
    )(place, fields, surface_kind)
    near = [packed[0]] + [move(packed[step], step, 0, lon_count) for step in (1, 2, 3)]
    far = [move(packed[4 + step], step, 1, lon_count) for step in range(4)]
    mine, other = gather_weights(mlp_up, mlp_down, lon_count)

    half_block = struct((WINDOWS * PADDED, D), bf16)
    encode = pl.pallas_call(
        functools.partial(encode_kernel, chunk=2),
        out_shape=half_block,
        in_specs=[SMEM, SMEM] + [VMEM] * 11,
        out_specs=VMEM,
        scratch_shapes=[
            pltpu.VMEM((HALF, 192, D), bf16),
            pltpu.VMEM((D // 128, WINDOWS * GROUP + 8, 128), f32),
        ],
        compiler_params=params(),
        name="encode",
    )

    def encoded(pieces):
        return encode(
            place,
            enc_scale,
            *pieces,
            patch_weight,
            level_embed,
            enc_gain.reshape(1, D),
            latent_query,
            kv_weight,
            enc_out_weight,
            kind_embed,
        )

    block1 = encoded(near)
    block0 = encoded(far)
    half_resid = struct((WINDOWS * PADDED, D), f32)
    resid0, resid1 = pl.pallas_call(
        window_kernel,
        out_shape=[half_resid] * 2,
        in_specs=[SMEM, SMEM] + [VMEM] * 5,
        out_specs=[VMEM] * 2,
        scratch_shapes=[pltpu.VMEM((WINDOWS * PADDED, 3 * D), bf16)] * 2
        + [pltpu.VMEM((WINDOWS * PADDED, D), bf16)] * 2,
        compiler_params=params(),
        name="window",
    )(place, swin_scale, block0, block1, attn_gain.reshape(1, D), qkv_weight, proj_weight)
    feed = pl.pallas_call(
        feed_kernel,
        out_shape=[half_block, struct((EDGE, D), bf16)],
        in_specs=[VMEM] * 4,
        out_specs=[VMEM] * 2,
        compiler_params=params(),
        name="feed",
    )
    gain = mlp_gain.reshape(1, D)
    out0, edge0 = feed(resid0, gain, mine, other)
    far_main = move(out0, 0, -1, lon_count)
    far_edge = move(edge0, -1, -1, lon_count)
    resid1, _ = lax.optimization_barrier((resid1, out0))
    out1, edge1 = feed(resid1, gain, mine, other)
    own_edge = move(edge1, -1, 0, lon_count)
    return pl.pallas_call(
        join_kernel,
        out_shape=struct((LATENT, ROWS, WW, D), bf16),
        in_specs=[VMEM] * 4,
        out_specs=VMEM,
        scratch_shapes=[pltpu.VMEM((WINDOWS * GROUP + 56, D), f32)] * 2,
        compiler_params=params(),
        name="join",
    )(out1, own_edge, far_main, far_edge)


def solution(mesh):
    return jax.shard_map(
        functools.partial(shards, mesh.shape["lon"]),
        mesh=mesh,
        in_specs=(
            P("lat", None, "lon"),
            P("lat", "lon"),
            P(),
            P(),
            P(),
            P(),
            P(),
            P(),
            P(),
            P(),
            P(),
            P(),
            P(),
            P(),
            P(),
            P(("lat", "lon"), None),
            P(("lat", "lon"), None),
        ),
        out_specs=P(None, "lat", "lon", None),
        check_vma=False,
    )
```

time: 662 us -> 122 us (0.18)
  waiting for transfers between devices: 370 us -> 32.3 us
  local copies, waits for them, and re-layouts: 163 us -> 7.29 us
  matrix products: 70.3 us -> 0 us
  Pallas kernels: 0 us -> 44.2 us
  other arithmetic: 22.8 us -> 0.01 us
  starting transfers between devices: 16.8 us -> 38.1 us
  between operations: 14 us -> 0.16 us
    all_gather x2 -> x0, waiting for transfers between devices: 349 us -> none  [the longest x1 305 us: shards(): lax.all_gather(mlp_down, ('lat', 'lon'), axis=0, tiled=True)]
    reshape x11 -> x0, local copies, waits for them, and re-layouts: 65.2 us -> none  [the longest x2 24.1 us: attend_windows(): projected.reshape(latent_count, row_windows, WH, col_windows, WW, 3, head...]
    dot_general x9 -> x0, matrix products: 58.1 us -> none  [the longest x1 20.3 us: grow_with(): return jnp.dot(hidden, pieces[1], preferred_element_type=jnp.float32)]
    pallas_call x0 -> x7, Pallas kernels: none -> 44.2 us  [the longest x2 18.7 us: encoded(): encode(place, enc_scale, *pieces, patch_weight, level_embed, enc_gain.res...]
    unnamed x37 -> x36, local copies, waits for them, and re-layouts: 43.4 us -> 4.57 us
    ppermute x4 -> x20, starting transfers between devices: 10.8 us -> 38.1 us  [the longest x10 16.5 us: move(): return lax.ppermute(array, ('lat', 'lon'), perm)]
    convert_element_type x5 -> x0, local copies, waits for them, and re-layouts: 25.9 us -> none  [the longest x1 10.1 us: encode_levels(): keyval = jnp.dot(level_tokens.reshape(level_count * patch_count, model_wi...]
    ppermute x4 -> x20, waiting for transfers between devices: 13.4 us -> 32.3 us  [the longest x3 20.6 us: gather_weights(): lax.ppermute(held, ('lat', 'lon'), [(a * lon_count + b, (a + 2 * far) % 4...]
  transfers between devices with their start and end apart: 7 -> 20, of which waited for: 6 -> 9; matrix products, arithmetic and copies ran while one was open for 35% -> 1% of each run, Pallas kernels for 0% -> 29%
where the time goes in v1:
time: 122 us
  Pallas kernels  44.2 us (36%)
  starting transfers between devices  38.1 us (31%)
  waiting for transfers between devices  32.3 us (26%)
  local copies, waits for them, and re-layouts  7.29 us (6%)
    ppermute x3, waiting for transfers between devices, gather_weights(): lax.ppermute(held, ('lat', 'lon'), [(a * lon_count + b, (a + 2 * far) % 4...  20.6 us
    pallas_call x2, Pallas kernels, encoded(): encode(place, enc_scale, *pieces, patch_weight, level_embed, enc_gain.res...  18.7 us
    ppermute x10, starting transfers between devices, move(): return lax.ppermute(array, ('lat', 'lon'), perm)  16.5 us
    ppermute x6, starting transfers between devices, gather_weights(): lax.ppermute(held, 'lon', [(i, i & ~bits | i + step * unit & bits) for i...  11.4 us
    pallas_call x1, Pallas kernels, shards(): pl.pallas_call(window_kernel, out_shape=[half_resid] * 2, in_specs=[SMEM,...  9.12 us
    ppermute x1, starting transfers between devices, gather_weights(): other = lax.ppermute(mine, 'lat', [(a, a ^ 1) for a in range(4)])  6.2 us
    ppermute x6, waiting for transfers between devices, gather_weights(): lax.ppermute(held, 'lon', [(i, i & ~bits | i + step * unit & bits) for i...  6.1 us
    pallas_call x1, Pallas kernels, shards(): out1, edge1 = feed(resid1, gain, mine, other)  5.8 us
  transfers between devices with their start and end apart: 20, of which 9 were waited for; matrix products, arithmetic and copies ran while one was open for 1% of the time, Pallas kernels for 29%

profile of v1, /device:TPU:1, one launch (start us, length us, event | category | flops | bytes accessed | tf_op | source)
XLA Modules:
  0.0 122.0 jit_solution(12210129920780678196)
XLA Ops:
  0.0 0.7 constant_dynamic-update-slice_fusion.9
  0.7 0.7 constant_dynamic-update-slice_fusion.8
  1.4 2.0 %collective-permute-start.7 = (bf16[16,1024]{1,0:T(8,128)(2,1)S(1)}, bf16[16,1024]{1,0:T(8,128)(2,1)S(1)}, u32[]{:S(2)}, u32[]{:S(2)}) collective-permute-start(bf16[16,1024]{1,0:T(8,128)(2,1)S(1)} %get-tuple-element.49), channel_id=1, source_target_pairs={{0,1},{1,2},{2,3},{3,0},{4,5},{5,6},{6,7},{7,4},{8,9},{9,10},{10,1... | collective-permute-start | bytes 98312 | tf_op jit(solution)/shard_map/ppermute | solution.py:293
  3.5 2.5 %collective-permute-start.8 = (bf16[16,1024]{1,0:T(8,128)(2,1)S(1)}, bf16[16,1024]{1,0:T(8,128)(2,1)S(1)}, u32[]{:S(2)}, u32[]{:S(2)}) collective-permute-start(bf16[16,1024]{1,0:T(8,128)(2,1)S(1)} %get-tuple-element.49), channel_id=1, source_target_pairs={{0,2},{1,3},{2,0},{3,1},{4,6},{5,7},{6,4},{7,5},{8,10},{9,11},{10,... | collective-permute-start | bytes 98312 | tf_op jit(solution)/shard_map/ppermute | solution.py:293
  5.9 1.2 collective-permute-start.9
  7.8 1.2 %collective-permute-done.9 = bf16[16,1024]{1,0:T(8,128)(2,1)S(1)} collective-permute-done((bf16[16,1024]{1,0:T(8,128)(2,1)S(1)}, bf16[16,1024]{1,0:T(8,128)(2,1)S(1)}, u32[]{:S(2)}, u32[]{:S(2)}) %collective-permute-start.9) | collective-permute-done | bytes 32800 | tf_op jit(solution)/shard_map/ppermute | solution.py:293
  9.0 1.7 %collective-permute-start.10 = (bf16[64,1024]{1,0:T(8,128)(2,1)S(1)}, bf16[64,1024]{1,0:T(8,128)(2,1)S(1)}, u32[]{:S(2)}, u32[]{:S(2)}) collective-permute-start(bf16[64,1024]{1,0:T(8,128)(2,1)S(1)} %pad_maximum_fusion), channel_id=1, source_target_pairs={{0,4},{1,5},{2,6},{3,7},{4,8},{5,9},{6,10},{7,11},{8,12},{9,13},{1... | collective-permute-start | bytes 393224 | tf_op jit(solution)/shard_map/ppermute | solution.py:293
  10.7 3.3 %collective-permute-start.11 = (bf16[64,1024]{1,0:T(8,128)(2,1)S(1)}, bf16[64,1024]{1,0:T(8,128)(2,1)S(1)}, u32[]{:S(2)}, u32[]{:S(2)}) collective-permute-start(bf16[64,1024]{1,0:T(8,128)(2,1)S(1)} %pad_maximum_fusion), channel_id=1, source_target_pairs={{0,8},{1,9},{2,10},{3,11},{4,12},{5,13},{6,14},{7,15},{8,0},{9,1},... | collective-permute-start | bytes 393224 | tf_op jit(solution)/shard_map/ppermute | solution.py:293
  14.0 0.7 collective-permute-start.12
  15.2 2.8 %collective-permute-done.11 = bf16[64,1024]{1,0:T(8,128)(2,1)S(1)} collective-permute-done((bf16[64,1024]{1,0:T(8,128)(2,1)S(1)}, bf16[64,1024]{1,0:T(8,128)(2,1)S(1)}, u32[]{:S(2)}, u32[]{:S(2)}) %collective-permute-start.11) | collective-permute-done | bytes 131104 | tf_op jit(solution)/shard_map/ppermute | solution.py:293
  18.1 0.9 collective-permute-done.12
  19.0 1.4 %collective-permute-start.13 = (bf16[256,1024]{1,0:T(8,128)(2,1)S(1)}, bf16[256,1024]{1,0:T(8,128)(2,1)S(1)}, u32[]{:S(2)}, u32[]{:S(2)}) collective-permute-start(bf16[256,1024]{1,0:T(8,128)(2,1)S(1)} %get-tuple-element.35), channel_id=1, source_target_pairs={{0,16},{1,17},{2,18},{3,19},{4,20},{5,21},{6,22},{7,23},{8,24},{9,... | collective-permute-start | bytes 1572872 | tf_op jit(solution)/shard_map/ppermute | solution.py:302
  20.4 2.6 %collective-permute-start.14 = (bf16[256,1024]{1,0:T(8,128)(2,1)S(1)}, bf16[256,1024]{1,0:T(8,128)(2,1)S(1)}, u32[]{:S(2)}, u32[]{:S(2)}) collective-permute-start(bf16[256,1024]{1,0:T(8,128)(2,1)S(1)} %get-tuple-element.35), channel_id=1, source_target_pairs={{0,64},{1,65},{2,66},{3,67},{4,68},{5,69},{6,70},{7,71},{8,72},{9,... | collective-permute-start | bytes 1572872 | tf_op jit(solution)/shard_map/ppermute | solution.py:302
  23.0 6.9 %collective-permute-done.13 = bf16[256,1024]{1,0:T(8,128)(2,1)S(1)} collective-permute-done((bf16[256,1024]{1,0:T(8,128)(2,1)S(1)}, bf16[256,1024]{1,0:T(8,128)(2,1)S(1)}, u32[]{:S(2)}, u32[]{:S(2)}) %collective-permute-start.13) | collective-permute-done | bytes 524320 | tf_op jit(solution)/shard_map/ppermute | solution.py:302
  30.0 13.7 %collective-permute-done.14 = bf16[256,1024]{1,0:T(8,128)(2,1)S(1)} collective-permute-done((bf16[256,1024]{1,0:T(8,128)(2,1)S(1)}, bf16[256,1024]{1,0:T(8,128)(2,1)S(1)}, u32[]{:S(2)}, u32[]{:S(2)}) %collective-permute-start.14) | collective-permute-done | bytes 524320 | tf_op jit(solution)/shard_map/ppermute | solution.py:302
  43.8 6.2 %collective-permute-start.16 = (bf16[1024,1024]{1,0:T(8,128)(2,1)S(1)}, bf16[1024,1024]{1,0:T(8,128)(2,1)}, u32[]{:S(2)}, u32[]{:S(2)}) collective-permute-start(bf16[1024,1024]{1,0:T(8,128)(2,1)S(1)} %constant_dynamic-update-slice_fusion.10.mine), channel_id=1, source_target_pairs={{0,32},{32,0},{64,96},{96,64},{1,33},{33,1},{65,97},{97,65},{2,34}... | collective-permute-start | bytes 6291464 | tf_op jit(solution)/shard_map/ppermute | solution.py:314
  50.0 0.7 copy.18.kind
  50.6 2.2 %pack.1 = (bf16[72,512]{1,0:T(8,128)(2,1)}, bf16[72,512]{1,0:T(8,128)(2,1)}, bf16[72,512]{1,0:T(8,128)(2,1)}, bf16[72,512]{1,0:T(8,128)(2,1)}, bf16[72,512]{1,0:...) custom-call(s32[1]{0:T(128)} %bitcast.place, ...), custom_call_target="tpu_custom_call" | custom-call | tf_op jit(solution)/shard_map/pack/pallas_call | solution.py:349
  52.8 3.1 %collective-permute-start.5 = (bf16[72,512]{1,0:T(8,128)(2,1)}, bf16[72,512]{1,0:T(8,128)(2,1)S(1)}, u32[]{:S(2)}, u32[]{:S(2)}) collective-permute-start(bf16[72,512]{1,0:T(8,128)(2,1)} %get-tuple-element.26), channel_id=1, source_target_pairs={{0,64},{1,65},{2,66},{3,67},{4,68},{5,69},{6,70},{7,71},{8,72},{9,... | collective-permute-start | bytes 221192 | tf_op jit(solution)/shard_map/ppermute | solution.py:324
  55.9 4.1 %collective-permute-start.1 = (bf16[72,512]{1,0:T(8,128)(2,1)}, bf16[72,512]{1,0:T(8,128)(2,1)S(1)}, u32[]{:S(2)}, u32[]{:S(2)}) collective-permute-start(bf16[72,512]{1,0:T(8,128)(2,1)} %get-tuple-element.21), channel_id=1, source_target_pairs={{0,33},{1,34},{2,35},{3,36},{4,37},{5,38},{6,39},{7,40},{8,41},{9,... | collective-permute-start | bytes 221192 | tf_op jit(solution)/shard_map/ppermute | solution.py:324
  60.0 1.7 %collective-permute-start.2 = (bf16[72,512]{1,0:T(8,128)(2,1)}, bf16[72,512]{1,0:T(8,128)(2,1)S(1)}, u32[]{:S(2)}, u32[]{:S(2)}) collective-permute-start(bf16[72,512]{1,0:T(8,128)(2,1)} %get-tuple-element.22), channel_id=1, source_target_pairs={{0,65},{1,66},{2,67},{3,68},{4,69},{5,70},{6,71},{7,72},{8,73},{9,... | collective-permute-start | bytes 221192 | tf_op jit(solution)/shard_map/ppermute | solution.py:324
  62.4 9.3 %encode.3.block1 = bf16[448,512]{1,0:T(8,128)(2,1)} custom-call(s32[1]{0:T(128)} %bitcast.place, f32[8]{0:T(128)} %enc_scale.3, bf16[72,512]{1,0:T(8,128)(2,1)} %get-tuple-element.24.piece0, bf16[72,512]{1,0:T(8,128)(2,1)} %copy-done.4, bf16[72,512]{1,0:T(8,128)(2,1)} %copy-done.5, bf16[72,512]{1,0:T(8,128)(2,1)} %copy-done.6, bf16[80,512]{1,0:T(8,128)(2,1)} %patch_weight.3, ...), custom_call_target="tpu_custom_call" | custom-call | tf_op jit(solution)/shard_map/encode/pallas_call | solution.py:377
  73.0 9.3 %encode.2.block0 = bf16[448,512]{1,0:T(8,128)(2,1)} custom-call(s32[1]{0:T(128)} %bitcast.place, f32[8]{0:T(128)} %enc_scale.3, bf16[72,512]{1,0:T(8,128)(2,1)} %copy-done.2, bf16[72,512]{1,0:T(8,128)(2,1)} %copy-done.3, bf16[72,512]{1,0:T(8,128)(2,1)} %copy-done.7, bf16[72,512]{1,0:T(8,128)(2,1)} %copy-done.8, bf16[80,512]{1,0:T(8,128)(2,1)} %patch_weight.3, ...), custom_call_target="tpu_custom_call" | custom-call | tf_op jit(solution)/shard_map/encode/pallas_call | solution.py:377
  82.4 9.1 %window.1 = (f32[448,512]{1,0:T(8,128)}, f32[448,512]{1,0:T(8,128)}) custom-call(s32[1]{0:T(128)} %bitcast.place, f32[8]{0:T(128)} %swin_scale.1, bf16[448,512]{1,0:T(8,128)(2,1)} %encode.2.block0, bf16[448,512]{1,0:T(8,128)(2,1)} %encode.3.block1, f32[1,512]{1,0:T(1,128)} %bitcast.8, bf16[512,1536]{1,0:T(8,128)(2,1)} %qkv_weight.1, bf16[512,512]{1,0:T(8,128)(2,1)} %proj_weight.1), custom_call_target="tpu_custom_call" | custom-call | tf_op jit(solution)/shard_map/window/pallas_call | solution.py:393
  91.5 5.8 %feed.2 = (bf16[448,512]{1,0:T(8,128)(2,1)}, bf16[64,512]{1,0:T(8,128)(2,1)}) custom-call(f32[448,512]{1,0:T(8,128)} %get-tuple-element.29.resid, f32[1,512]{1,0:T(1,128)} %bitcast.6, bf16[1024,1024]{1,0:T(8,128)(2,1)} %copy-done, bf16[1024,1024]{1,0:T(8,128)(2,1)} %collective-permute-done.16.other), custom_call_target="tpu_custom_call" | custom-call | tf_op jit(solution)/shard_map/feed/pallas_call | solution.py:412
  97.3 3.7 %collective-permute-start.18 = (bf16[448,512]{1,0:T(8,128)(2,1)}, bf16[448,512]{1,0:T(8,128)(2,1)S(1)}, u32[]{:S(2)}, u32[]{:S(2)}) collective-permute-start(bf16[448,512]{1,0:T(8,128)(2,1)} %get-tuple-element.30), channel_id=1, source_target_pairs={{0,31},{1,0},{2,1},{3,2},{4,3},{5,4},{6,5},{7,6},{8,7},{9,8},{10,9... | collective-permute-start | bytes 1376264 | tf_op jit(solution)/shard_map/ppermute | solution.py:324
  101.0 5.8 %feed.3 = (bf16[448,512]{1,0:T(8,128)(2,1)}, bf16[64,512]{1,0:T(8,128)(2,1)}) custom-call(f32[448,512]{1,0:T(8,128)} %get-tuple-element.31.resid, f32[1,512]{1,0:T(1,128)} %bitcast.7, bf16[1024,1024]{1,0:T(8,128)(2,1)} %copy-done, bf16[1024,1024]{1,0:T(8,128)(2,1)} %collective-permute-done.16.other), custom_call_target="tpu_custom_call" | custom-call | tf_op jit(solution)/shard_map/feed/pallas_call | solution.py:416
  106.8 2.9 %collective-permute-start.17 = (bf16[64,512]{1,0:T(8,128)(2,1)}, bf16[64,512]{1,0:T(8,128)(2,1)S(1)}, u32[]{:S(2)}, u32[]{:S(2)}) collective-permute-start(bf16[64,512]{1,0:T(8,128)(2,1)} %get-tuple-element.33), channel_id=1, source_target_pairs={{0,96},{1,97},{2,98},{3,99},{4,100},{5,101},{6,102},{7,103},{8,104... | collective-permute-start | bytes 196616 | tf_op jit(solution)/shard_map/ppermute | solution.py:324
  110.3 3.0 %collective-permute-done.17.own_edge = bf16[64,512]{1,0:T(8,128)(2,1)S(1)} collective-permute-done((bf16[64,512]{1,0:T(8,128)(2,1)}, bf16[64,512]{1,0:T(8,128)(2,1)S(1)}, u32[]{:S(2)}, u32[]{:S(2)}) %collective-permute-start.17) | collective-permute-done | bytes 65568 | tf_op jit(solution)/shard_map/ppermute | solution.py:324
  113.2 2.6 %collective-permute-done.19.far_edge = bf16[64,512]{1,0:T(8,128)(2,1)S(1)} collective-permute-done((bf16[64,512]{1,0:T(8,128)(2,1)S(1)}, bf16[64,512]{1,0:T(8,128)(2,1)S(1)}, u32[]{:S(2)}, u32[]{:S(2)}) %collective-permute-start.19) | collective-permute-done | bytes 65568 | tf_op jit(solution)/shard_map/ppermute | solution.py:324
  116.7 2.6 %join.1 = bf16[3,24,12,512]{3,2,1,0:T(8,128)(2,1)} custom-call(bf16[448,512]{1,0:T(8,128)(2,1)} %get-tuple-element.32.own, bf16[64,512]{1,0:T(8,128)(2,1)} %copy-done.9, bf16[448,512]{1,0:T(8,128)(2,1)} %copy-done.1, bf16[64,512]{1,0:T(8,128)(2,1)} %copy-done.10), custom_call_target="tpu_custom_call" | custom-call | tf_op jit(solution)/shard_map/join/pallas_call | solution.py:418
  119.3 2.7 %copy.19 = bf16[3,24,12,512]{3,1,2,0:T(8,128)(2,1)} copy(bf16[3,24,12,512]{3,2,1,0:T(8,128)(2,1)} %join.1) | data formatting | bytes 1769472 | tf_op jit(solution)/shard_map/join/pallas_call | solution.py:418
  (55 shorter events, 4.6 us)
Async XLA Ops:
  1.4 5.6 %collective-permute-start.7 = (bf16[16,1024]{1,0:T(8,128)(2,1)S(1)}, bf16[16,1024]{1,0:T(8,128)(2,1)S(1)}, u32[]{:S(2)}, u32[]{:S(2)}) collective-permute-start(bf16[16,1024]{1,0:T(8,128)(2,1)S(1)} %get-tuple-element.49), channel_id=1, source_target_pairs={{0,1},{1,2},{2,3},{3,0},{4,5},{5,6},{6,7},{7,4},{8,9},{9,10},{10,1... | collective-permute-start | bytes 98312 | tf_op jit(solution)/shard_map/ppermute | solution.py:293
  3.5 4.3 %collective-permute-start.8 = (bf16[16,1024]{1,0:T(8,128)(2,1)S(1)}, bf16[16,1024]{1,0:T(8,128)(2,1)S(1)}, u32[]{:S(2)}, u32[]{:S(2)}) collective-permute-start(bf16[16,1024]{1,0:T(8,128)(2,1)S(1)} %get-tuple-element.49), channel_id=1, source_target_pairs={{0,2},{1,3},{2,0},{3,1},{4,6},{5,7},{6,4},{7,5},{8,10},{9,11},{10,... | collective-permute-start | bytes 98312 | tf_op jit(solution)/shard_map/ppermute | solution.py:293
  5.9 3.1 %collective-permute-start.9 = (bf16[16,1024]{1,0:T(8,128)(2,1)S(1)}, bf16[16,1024]{1,0:T(8,128)(2,1)S(1)}, u32[]{:S(2)}, u32[]{:S(2)}) collective-permute-start(bf16[16,1024]{1,0:T(8,128)(2,1)S(1)} %get-tuple-element.49), channel_id=1, source_target_pairs={{0,3},{1,0},{2,1},{3,2},{4,7},{5,4},{6,5},{7,6},{8,11},{9,8},{10,9... | collective-permute-start | bytes 98312 | tf_op jit(solution)/shard_map/ppermute | solution.py:293
  9.0 6.2 %collective-permute-start.10 = (bf16[64,1024]{1,0:T(8,128)(2,1)S(1)}, bf16[64,1024]{1,0:T(8,128)(2,1)S(1)}, u32[]{:S(2)}, u32[]{:S(2)}) collective-permute-start(bf16[64,1024]{1,0:T(8,128)(2,1)S(1)} %pad_maximum_fusion), channel_id=1, source_target_pairs={{0,4},{1,5},{2,6},{3,7},{4,8},{5,9},{6,10},{7,11},{8,12},{9,13},{1... | collective-permute-start | bytes 393224 | tf_op jit(solution)/shard_map/ppermute | solution.py:293
  10.7 7.3 %collective-permute-start.11 = (bf16[64,1024]{1,0:T(8,128)(2,1)S(1)}, bf16[64,1024]{1,0:T(8,128)(2,1)S(1)}, u32[]{:S(2)}, u32[]{:S(2)}) collective-permute-start(bf16[64,1024]{1,0:T(8,128)(2,1)S(1)} %pad_maximum_fusion), channel_id=1, source_target_pairs={{0,8},{1,9},{2,10},{3,11},{4,12},{5,13},{6,14},{7,15},{8,0},{9,1},... | collective-permute-start | bytes 393224 | tf_op jit(solution)/shard_map/ppermute | solution.py:293
  14.0 5.0 %collective-permute-start.12 = (bf16[64,1024]{1,0:T(8,128)(2,1)S(1)}, bf16[64,1024]{1,0:T(8,128)(2,1)S(1)}, u32[]{:S(2)}, u32[]{:S(2)}) collective-permute-start(bf16[64,1024]{1,0:T(8,128)(2,1)S(1)} %pad_maximum_fusion), channel_id=1, source_target_pairs={{0,12},{1,13},{2,14},{3,15},{4,0},{5,1},{6,2},{7,3},{8,4},{9,5},{1... | collective-permute-start | bytes 393224 | tf_op jit(solution)/shard_map/ppermute | solution.py:293
  15.2 34.8 %copy-start.11 = (s32[24,12]{0,1:T(8,128)S(1)}, s32[24,12]{0,1:T(8,128)}, u32[]{:S(2)}) copy-start(s32[24,12]{0,1:T(8,128)} %param.18) | copy-start | bytes 3460
  19.0 10.9 %collective-permute-start.13 = (bf16[256,1024]{1,0:T(8,128)(2,1)S(1)}, bf16[256,1024]{1,0:T(8,128)(2,1)S(1)}, u32[]{:S(2)}, u32[]{:S(2)}) collective-permute-start(bf16[256,1024]{1,0:T(8,128)(2,1)S(1)} %get-tuple-element.35), channel_id=1, source_target_pairs={{0,16},{1,17},{2,18},{3,19},{4,20},{5,21},{6,22},{7,23},{8,24},{9,... | collective-permute-start | bytes 1572872 | tf_op jit(solution)/shard_map/ppermute | solution.py:302
  20.4 23.2 %collective-permute-start.14 = (bf16[256,1024]{1,0:T(8,128)(2,1)S(1)}, bf16[256,1024]{1,0:T(8,128)(2,1)S(1)}, u32[]{:S(2)}, u32[]{:S(2)}) collective-permute-start(bf16[256,1024]{1,0:T(8,128)(2,1)S(1)} %get-tuple-element.35), channel_id=1, source_target_pairs={{0,64},{1,65},{2,66},{3,67},{4,68},{5,69},{6,70},{7,71},{8,72},{9,... | collective-permute-start | bytes 1572872 | tf_op jit(solution)/shard_map/ppermute | solution.py:302
  23.0 20.7 %collective-permute-start.15 = (bf16[256,1024]{1,0:T(8,128)(2,1)S(1)}, bf16[256,1024]{1,0:T(8,128)(2,1)S(1)}, u32[]{:S(2)}, u32[]{:S(2)}) collective-permute-start(bf16[256,1024]{1,0:T(8,128)(2,1)S(1)} %get-tuple-element.35), channel_id=1, source_target_pairs={{0,80},{1,81},{2,82},{3,83},{4,84},{5,85},{6,86},{7,87},{8,88},{9,... | collective-permute-start | bytes 1572872 | tf_op jit(solution)/shard_map/ppermute | solution.py:302
  43.7 38.6 %copy-start = (bf16[1024,1024]{1,0:T(8,128)(2,1)}, bf16[1024,1024]{1,0:T(8,128)(2,1)S(1)}, u32[]{:S(2)}) copy-start(bf16[1024,1024]{1,0:T(8,128)(2,1)S(1)} %constant_dynamic-update-slice_fusion.10.mine) | copy-start | bytes 6291460
  43.8 47.7 %collective-permute-start.16 = (bf16[1024,1024]{1,0:T(8,128)(2,1)S(1)}, bf16[1024,1024]{1,0:T(8,128)(2,1)}, u32[]{:S(2)}, u32[]{:S(2)}) collective-permute-start(bf16[1024,1024]{1,0:T(8,128)(2,1)S(1)} %constant_dynamic-update-slice_fusion.10.mine), channel_id=1, source_target_pairs={{0,32},{32,0},{64,96},{96,64},{1,33},{33,1},{65,97},{97,65},{2,34}... | collective-permute-start | bytes 6291464 | tf_op jit(solution)/shard_map/ppermute | solution.py:314
  52.8 3.1 %collective-permute-start.4 = (bf16[72,512]{1,0:T(8,128)(2,1)}, bf16[72,512]{1,0:T(8,128)(2,1)S(1)}, u32[]{:S(2)}, u32[]{:S(2)}) collective-permute-start(bf16[72,512]{1,0:T(8,128)(2,1)} %get-tuple-element.25), channel_id=1, source_target_pairs={{0,32},{1,33},{2,34},{3,35},{4,36},{5,37},{6,38},{7,39},{8,40},{9,... | collective-permute-start | bytes 221192 | tf_op jit(solution)/shard_map/ppermute | solution.py:324
  52.8 7.2 %collective-permute-start.5 = (bf16[72,512]{1,0:T(8,128)(2,1)}, bf16[72,512]{1,0:T(8,128)(2,1)S(1)}, u32[]{:S(2)}, u32[]{:S(2)}) collective-permute-start(bf16[72,512]{1,0:T(8,128)(2,1)} %get-tuple-element.26), channel_id=1, source_target_pairs={{0,64},{1,65},{2,66},{3,67},{4,68},{5,69},{6,70},{7,71},{8,72},{9,... | collective-permute-start | bytes 221192 | tf_op jit(solution)/shard_map/ppermute | solution.py:324
  55.9 5.8 %collective-permute-start.6 = (bf16[72,512]{1,0:T(8,128)(2,1)}, bf16[72,512]{1,0:T(8,128)(2,1)S(1)}, u32[]{:S(2)}, u32[]{:S(2)}) collective-permute-start(bf16[72,512]{1,0:T(8,128)(2,1)} %get-tuple-element.27), channel_id=1, source_target_pairs={{0,96},{1,97},{2,98},{3,99},{4,100},{5,101},{6,102},{7,103},{8,104... | collective-permute-start | bytes 221192 | tf_op jit(solution)/shard_map/ppermute | solution.py:324
  55.9 15.8 %collective-permute-start = (bf16[72,512]{1,0:T(8,128)(2,1)}, bf16[72,512]{1,0:T(8,128)(2,1)S(1)}, u32[]{:S(2)}, u32[]{:S(2)}) collective-permute-start(bf16[72,512]{1,0:T(8,128)(2,1)} %get-tuple-element.20), channel_id=1, source_target_pairs={{0,1},{1,2},{2,3},{3,4},{4,5},{5,6},{6,7},{7,8},{8,9},{9,10},{10,1... | collective-permute-start | bytes 221192 | tf_op jit(solution)/shard_map/ppermute | solution.py:324
  55.9 6.2 %copy-start.4 = (bf16[72,512]{1,0:T(8,128)(2,1)}, bf16[72,512]{1,0:T(8,128)(2,1)S(1)}, u32[]{:S(2)}) copy-start(bf16[72,512]{1,0:T(8,128)(2,1)S(1)} %collective-permute-done.4.piece1) | copy-start | bytes 221188
  55.9 15.8 %collective-permute-start.1 = (bf16[72,512]{1,0:T(8,128)(2,1)}, bf16[72,512]{1,0:T(8,128)(2,1)S(1)}, u32[]{:S(2)}, u32[]{:S(2)}) collective-permute-start(bf16[72,512]{1,0:T(8,128)(2,1)} %get-tuple-element.21), channel_id=1, source_target_pairs={{0,33},{1,34},{2,35},{3,36},{4,37},{5,38},{6,39},{7,40},{8,41},{9,... | collective-permute-start | bytes 221192 | tf_op jit(solution)/shard_map/ppermute | solution.py:324
  60.0 2.1 %copy-start.5 = (bf16[72,512]{1,0:T(8,128)(2,1)}, bf16[72,512]{1,0:T(8,128)(2,1)S(1)}, u32[]{:S(2)}) copy-start(bf16[72,512]{1,0:T(8,128)(2,1)S(1)} %collective-permute-done.5.piece2) | copy-start | bytes 221188
  60.0 11.7 %collective-permute-start.2 = (bf16[72,512]{1,0:T(8,128)(2,1)}, bf16[72,512]{1,0:T(8,128)(2,1)S(1)}, u32[]{:S(2)}, u32[]{:S(2)}) collective-permute-start(bf16[72,512]{1,0:T(8,128)(2,1)} %get-tuple-element.22), channel_id=1, source_target_pairs={{0,65},{1,66},{2,67},{3,68},{4,69},{5,70},{6,71},{7,72},{8,73},{9,... | collective-permute-start | bytes 221192 | tf_op jit(solution)/shard_map/ppermute | solution.py:324
  61.7 0.6 copy-start.6
  61.7 10.0 %collective-permute-start.3 = (bf16[72,512]{1,0:T(8,128)(2,1)}, bf16[72,512]{1,0:T(8,128)(2,1)S(1)}, u32[]{:S(2)}, u32[]{:S(2)}) collective-permute-start(bf16[72,512]{1,0:T(8,128)(2,1)} %get-tuple-element.23), channel_id=1, source_target_pairs={{0,97},{1,98},{2,99},{3,100},{4,101},{5,102},{6,103},{7,104},{8,10... | collective-permute-start | bytes 221192 | tf_op jit(solution)/shard_map/ppermute | solution.py:324
  71.7 0.7 copy-start.3
  71.7 0.7 copy-start.7
  72.4 0.6 copy-start.8
  97.3 18.6 %collective-permute-start.18 = (bf16[448,512]{1,0:T(8,128)(2,1)}, bf16[448,512]{1,0:T(8,128)(2,1)S(1)}, u32[]{:S(2)}, u32[]{:S(2)}) collective-permute-start(bf16[448,512]{1,0:T(8,128)(2,1)} %get-tuple-element.30), channel_id=1, source_target_pairs={{0,31},{1,0},{2,1},{3,2},{4,3},{5,4},{6,5},{7,6},{8,7},{9,8},{10,9... | collective-permute-start | bytes 1376264 | tf_op jit(solution)/shard_map/ppermute | solution.py:324
  101.0 8.8 %copy-start.12 = (bf16[64,512]{1,0:T(8,128)(2,1)S(1)}, bf16[64,512]{1,0:T(8,128)(2,1)}, u32[]{:S(2)}) copy-start(bf16[64,512]{1,0:T(8,128)(2,1)} %get-tuple-element.34) | copy-start | bytes 196612
  106.8 6.4 %collective-permute-start.17 = (bf16[64,512]{1,0:T(8,128)(2,1)}, bf16[64,512]{1,0:T(8,128)(2,1)S(1)}, u32[]{:S(2)}, u32[]{:S(2)}) collective-permute-start(bf16[64,512]{1,0:T(8,128)(2,1)} %get-tuple-element.33), channel_id=1, source_target_pairs={{0,96},{1,97},{2,98},{3,99},{4,100},{5,101},{6,102},{7,103},{8,104... | collective-permute-start | bytes 196616 | tf_op jit(solution)/shard_map/ppermute | solution.py:324
  109.8 6.1 %collective-permute-start.19 = (bf16[64,512]{1,0:T(8,128)(2,1)S(1)}, bf16[64,512]{1,0:T(8,128)(2,1)S(1)}, u32[]{:S(2)}, u32[]{:S(2)}) collective-permute-start(bf16[64,512]{1,0:T(8,128)(2,1)S(1)} %copy-done.12), channel_id=1, source_target_pairs={{0,127},{1,96},{2,97},{3,98},{4,99},{5,100},{6,101},{7,102},{8,103... | collective-permute-start | bytes 196616 | tf_op jit(solution)/shard_map/ppermute | solution.py:324
  113.2 2.6 %copy-start.9 = (bf16[64,512]{1,0:T(8,128)(2,1)}, bf16[64,512]{1,0:T(8,128)(2,1)S(1)}, u32[]{:S(2)}) copy-start(bf16[64,512]{1,0:T(8,128)(2,1)S(1)} %collective-permute-done.17.own_edge) | copy-start | bytes 196612
  115.9 0.6 copy-start.10
  115.9 0.8 copy-start.1
  (1 other events, 0.6 us)
